TPU v7x, 32 devices: a whole 2x2x4 slice. The times are simulated.
32 devices in a mesh: grp: 2 (over core), ctx: 8 (over z, y), wsh: 2 (over x).
Axes of the slice: x: 2, y: 2, z: 4, core: 2. Of those that a mesh axis runs over, the one named last changes fastest.
Arguments:
- stream: bfloat16 [2, 2, 3072, 512], P('grp', 'wsh', 'ctx'), may hold values from -6 to 6
- memory: bfloat16 [2, 2, 1024, 512], P('grp', 'wsh', 'ctx'), may hold values from -6 to 6
- cotangent: bfloat16 [2, 2, 3072, 512], P('grp', 'wsh', 'ctx'), may hold values from -6 to 6
- deal_order: int32 [2, 2, 24], P('grp', 'wsh'), may hold values from 0 to 23, each once within a row
- offsets: int32 [2, 2, 1], P('grp', 'wsh'), may hold values from 128 to 1024
- context_mask: int32 [2, 2, 16, 8], P('grp', 'wsh'), may hold values 0 or 1
- w_qkv: bfloat16 [512, 1536], replicated, may hold values from -0.25 to 0.25
- w_out: bfloat16 [512, 512], replicated, may hold values from -3 to 3
- w_cq: bfloat16 [512, 512], replicated, may hold values from -0.25 to 0.25
- w_ckv: bfloat16 [512, 1024], replicated, may hold values from -0.25 to 0.25
- w_cout: bfloat16 [512, 512], replicated, may hold values from -3 to 3
- w_up: bfloat16 [512, 2048], replicated, may hold values from -0.25 to 0.25
- w_down: bfloat16 [2048, 512], replicated, may hold values from -0.125 to 0.125
- b_up: float32 [2048], replicated, may hold values from -3 to 3
- gains: float32 [3, 512], replicated, may hold values from 0.5 to 1.5
- biases: float32 [10, 512], replicated, may hold values from -3 to 3
Outputs:
- output: float32 [2, 2, 3072, 512], P('grp', 'wsh', 'ctx')
- grad_stream: float32 [2, 2, 3072, 512], P('grp', 'wsh', 'ctx')
- grad_memory: float32 [2, 2, 1024, 512], P('grp', 'wsh', 'ctx')
- grad_w_qkv: float32 [512, 1536], P(('ctx', 'wsh'))
- grad_w_out: float32 [512, 512], P(('ctx', 'wsh'))
- grad_w_cq: float32 [512, 512], P(('ctx', 'wsh'))
- grad_w_ckv: float32 [512, 1024], P(('ctx', 'wsh'))
- grad_w_cout: float32 [512, 512], P(('ctx', 'wsh'))
- grad_w_up: float32 [512, 2048], P(('ctx', 'wsh'))
- grad_w_down: float32 [2048, 512], P(('ctx', 'wsh'))
- grad_b_up: float32 [2048], P(('ctx', 'wsh'))
- grad_gains: float32 [3, 512], P(None, ('ctx', 'wsh'))
- grad_biases: float32 [10, 512], P(None, ('ctx', 'wsh'))
Inputs may be any that keep to these rules, and one draw needn't show every extreme that they name: `deal_order`: each family's row is a permutation of the block numbers 0 to 23.
All inputs are finite; a program needn't handle non-finite values. No bound on the sum of `context_mask` on one device may be relied on, other than what follows from the above.
Results may differ from a plain program's by a relative error of at most 0.025.
Values may be sent and summed in bfloat16 or wider, within the bound.
A program may use at most 320 MiB of HBM per device.

v0:
```python
import functools

import jax
import jax.numpy as jnp
from jax import lax
from jax.experimental import pallas as pl
from jax.experimental.pallas import tpu as pltpu
from jax.sharding import PartitionSpec as P

HEADS = 8
BLK = 128
CBLK = 16


NEG_FILL = -1000000000.0
EPS_NORM = 1e-05


MESH_ID = pl.DeviceIdType.MESH
TILE = 512
STEP = 256
KEYS = 1024
BIG_VMEM = 62 << 20
LOW = jnp.bfloat16
WIDE = jnp.float32
SHARDS = 16
HALF = 16
ROWS = 4
PIECES = dict(
    up0=1024, up1=1024, down0=1024, down1=1024, cross=1024, out=512, ckv=1024, wq=512, wk=512, wv=512
)
TURNS = dict(up0=0, up1=1, down0=0, down1=1, cross=0, out=0, ckv=0, wq=2, wk=2, wv=2)
FEW_ROWS = 24


def nn(left, right):
    return lax.dot_general(
        left, right, (((1,), (0,)), ((), ())), preferred_element_type=WIDE
    )


def nt(left, right):
    return lax.dot_general(
        left, right, (((1,), (1,)), ((), ())), preferred_element_type=WIDE
    )


def swap(block):
    return block.astype(WIDE).T.astype(block.dtype)


def plus(left, right):
    return left.astype(WIDE) + right.astype(WIDE)


def column_sums(values):
    return jnp.sum(values.astype(WIDE), axis=0, keepdims=True)


def norm_parts(values):
    center = values - jnp.mean(values, axis=-1, keepdims=True)
    spread = jnp.mean(center * center, axis=-1, keepdims=True)
    scale = lax.rsqrt(spread + EPS_NORM)
    return center * scale, scale


def norm_pull(unit, scale, gain, upstream):
    inner = upstream * gain
    first = jnp.mean(inner, axis=-1, keepdims=True)
    second = jnp.mean(inner * unit, axis=-1, keepdims=True)
    return scale * (inner - first - unit * second)


def hide_later(scores, lead):
    rows = lax.broadcasted_iota(jnp.int32, scores.shape, 0)
    cols = lax.broadcasted_iota(jnp.int32, scores.shape, 1)
    return jnp.where(rows - cols <= lead, scores, NEG_FILL)


def hide_prompt(scores, offset_ref, open_ref, tile, chunk, prompt_blocks):
    span, key_span = TILE // BLK, scores.shape[0] // BLK
    rows = lax.broadcasted_iota(jnp.int32, (BLK, BLK), 0)
    columns = []
    for q_sub in range(span):
        pieces = []
        for k_sub in range(key_span):
            key_block = chunk * key_span + k_sub
            opened = open_ref[tile * span + q_sub - prompt_blocks, key_block]
            opened = jnp.where(key_block == 0, 1, opened)
            limit = jnp.where(opened > 0, offset_ref[0], 0) - key_block * BLK
            part = scores[k_sub * BLK : (k_sub + 1) * BLK, q_sub * BLK : (q_sub + 1) * BLK]
            pieces.append(jnp.where(rows < limit, part, NEG_FILL))
        columns.append(jnp.concatenate(pieces, axis=0))
    return jnp.concatenate(columns, axis=1)


def apart(upper, lower):
    none = jnp.zeros_like(upper)
    return jnp.concatenate(
        [jnp.concatenate([upper, none], axis=1), jnp.concatenate([none, lower], axis=1)], axis=0
    )


def apart_columns(pair):
    lanes = lax.broadcasted_iota(jnp.int32, pair.shape, 1)
    wide = pair.astype(WIDE)
    left = jnp.where(lanes < pair.shape[1] // 2, wide, 0.0).astype(pair.dtype)
    right = jnp.where(lanes < pair.shape[1] // 2, 0.0, wide).astype(pair.dtype)
    return jnp.concatenate([left, right], axis=0)


def remote(src_ref, dst_ref, send_sem, recv_sem, target):
    return pltpu.make_async_remote_copy(
        src_ref=src_ref,
        dst_ref=dst_ref,
        send_sem=send_sem,
        recv_sem=recv_sem,
        device_id=target,
        device_id_type=MESH_ID,
    )


class Bag:
    def __init__(self, items):
        self.__dict__.update(items)


class Spot:
    def __init__(self):
        ctx = lax.axis_index("ctx")
        self.grp, self.ctx, self.wsh = lax.axis_index("grp"), ctx, lax.axis_index("wsh")
        self.row, self.col = ctx // 2, lax.rem(ctx, 2)
        self.core_peer = (1 - self.grp, ctx, self.wsh)
        self.wsh_peer = (self.grp, ctx, 1 - self.wsh)
        self.col_peer = self.at_row_col(self.row, 1 - self.col)
        self.cross_peer = (self.grp, self.row * 2 + 1 - self.col, 1 - self.wsh)
        self.rows_by_step = [lax.rem(self.row + step, ROWS) for step in range(ROWS)]
        self.row_peers = [self.at_row_col(row, self.col) for row in self.rows_by_step]
        self.far_peers = [(1 - self.grp, peer[1], self.wsh) for peer in self.row_peers]
        self.ways = [
            (self.wsh_peer, self.col, 1 - self.wsh),
            (self.col_peer, 1 - self.col, self.wsh),
            (self.cross_peer, 1 - self.col, 1 - self.wsh),
        ]
        self.ctx_by_step = [lax.rem(ctx + step, HEADS) for step in range(HEADS)]
        self.ctx_peers = [(self.grp, peer, self.wsh) for peer in self.ctx_by_step]

    def at_row_col(self, row, col):
        return (self.grp, row * 2 + col, self.wsh)

    def greet(self):
        barrier = pltpu.get_barrier_semaphore()
        targets = [self.core_peer, self.wsh_peer, self.cross_peer]
        targets += self.ctx_peers[1:] + self.far_peers[1:]
        for target in targets:
            pl.semaphore_signal(barrier, inc=1, device_id=target, device_id_type=MESH_ID)
        return len(targets)


class Exchange:
    def __init__(self, spot, source, sems, parts):
        self.spot, self.source, self.sems, self.parts = spot, source, sems, parts
        self.copies = [[] for _ in parts]

    def start(self, part=0):
        spot, own_blocks = self.spot, self.source.shape[1]
        first, count, rows, target, target_rows = self.parts[part]
        here = (pl.ds(spot.ctx * own_blocks + first, count), target_rows)
        there = (pl.ds(first, count), rows)
        for step in range(1, HEADS):
            copy = remote(
                self.source.at[(spot.ctx_by_step[step],) + there], target.at[here],
                self.sems.at[0, step, part], self.sems.at[1, step, part], spot.ctx_peers[step],
            )
            copy.start()
            self.copies[part].append(copy)
        target[here] = self.source[(spot.ctx,) + there]

    def wait(self, part=0):
        for copy in self.copies[part]:
            copy.wait()


class Piece:
    def __init__(self, spot, turn, refs, outs):
        self.spot, self.turn, self.sems, self.outs = spot, turn, refs.sems, outs
        self.part, self.core_land, self.hop_land = refs.part, refs.core_land, refs.hop_land
        self.turn_land, self.row_land = refs.turn_land, refs.row_land
        self.turn_sum = self.core_land.at[:, 0]
        self.copies = []
        self.stage = 0

    def copy(self, index, source, target_ref, target):
        copy = remote(source, target_ref, self.sems.at[0, index], self.sems.at[1, index], target)
        copy.start()
        self.copies.append(copy)

    def finish(self):
        for copy in self.copies:
            copy.wait()
        self.copies = []

    def send_rows(self):
        spot = self.spot
        for step in range(1, ROWS):
            self.copy(
                2 + step, self.turn_land.at[spot.rows_by_step[step]],
                self.row_land.at[step - 1], spot.row_peers[step],
            )

    def steps(self, stage):
        while self.stage < stage:
            self.step()

    def step(self):
        spot, part = self.spot, self.part
        own = spot.grp
        if self.stage == 0:
            self.copy(0, part.at[1 - own], self.core_land, spot.core_peer)
        elif self.stage == 1:
            self.finish()
            part[own] = plus(part[own], self.core_land[...]).astype(LOW)
            if self.turn == 2:
                for way, (target, to_col, to_wsh) in enumerate(spot.ways):
                    self.copy(
                        1 + way, part.at[own, :, to_col, to_wsh], self.hop_land.at[way],
                        target,
                    )
            elif self.turn == 0:
                self.copy(1, part.at[own, :, :, 1 - spot.wsh], self.hop_land, spot.wsh_peer)
            else:
                self.copy(1, part.at[own, :, 1 - spot.col], self.hop_land, spot.col_peer)
        elif self.stage == 2:
            self.finish()
            if self.turn == 2:
                total = part[own, :, spot.col, spot.wsh].astype(WIDE)
                for way in range(3):
                    total = total + self.hop_land[way].astype(WIDE)
                self.turn_land[...] = total.astype(LOW)
                self.row_land[own, spot.row] = self.turn_land[spot.row]
                for step in range(ROWS):
                    for side, peers in enumerate((spot.row_peers, spot.far_peers)):
                        if step + side > 0:
                            self.copy(
                                4 + 2 * step + side, self.turn_land.at[spot.rows_by_step[step]],
                                self.row_land.at[own, spot.row], peers[step],
                            )
                self.stage = 4
                return
            if self.turn == 0:
                mine = part[own, :, :, spot.wsh]
                away, target = 1 - spot.col, spot.col_peer
            else:
                mine = part[own, :, spot.col]
                away, target = 1 - spot.wsh, spot.wsh_peer
            self.turn_sum[...] = plus(mine, self.hop_land[...]).astype(LOW)
            self.copy(2, self.turn_sum.at[:, away], self.turn_land, target)
        elif self.stage == 3:
            self.finish()
            keep = spot.col if self.turn == 0 else spot.wsh
            self.turn_land[...] = plus(self.turn_sum[:, keep], self.turn_land[...]).astype(LOW)
            self.send_rows()
        elif self.stage == 4:
            self.finish()
            if self.turn == 2:
                (out_ref, _, column, width), = self.outs
                for half in range(2):
                    total = self.row_land[half, 0].astype(WIDE)
                    for row in range(1, ROWS):
                        total = total + self.row_land[half, row].astype(WIDE)
                    out_ref[half * HALF : (half + 1) * HALF, column : column + width] = total
                self.stage = 6
                return
            total = self.turn_land[spot.row].astype(WIDE)
            for step in range(ROWS - 1):
                total = total + self.row_land[step].astype(WIDE)
            at = 0
            for index, (out_ref, row, column, width) in enumerate(self.outs):
                here = (
                    pl.ds(pl.multiple_of(row + own * HALF, HALF), HALF),
                    slice(column, column + width),
                )
                out_ref[here] = total[:, at : at + width]
                at += width
                self.copy(7 + index, out_ref.at[here], out_ref.at[here], spot.core_peer)
        elif self.stage == 5:
            self.finish()
        self.stage += 1


def layer_kernel(
    prompt_blocks,
    deal_ref, offset_ref, open_ref, tokens_ref, memory_ref, cot_ref,
    w_qkv_hbm, w_out_hbm, w_cq_hbm, w_ckv_hbm, w_cout_hbm, w_up_hbm, w_down_hbm,
    b_up_ref, gains_ref, biases_ref,
    output_ref, g_stream_ref, g_memory_ref, o_qkv_ref, o_out_ref, o_cq_ref, o_ckv_ref, o_cout_ref,
    o_up_ref, o_down_ref, o_b_up_ref, o_gains_ref, o_biases_ref,
    refs,
):
    spot = Spot()
    greeted = spot.greet()
    row_count, width = tokens_ref.shape
    own_blocks = row_count // BLK
    head = width // HEADS
    blocks = own_blocks * HEADS
    mem_rows = memory_ref.shape[0]
    mem_total = mem_rows * HEADS
    hidden_width = b_up_ref.shape[1]
    chunks = hidden_width // width
    pairs = HEADS // 2
    score_scale = head ** (-0.5)
    prompt_tiles = prompt_blocks * BLK // TILE
    tiles = blocks * BLK // TILE

    sources = dict(
        w_qkv=w_qkv_hbm, w_ckv=w_ckv_hbm, w_out=w_out_hbm, w_cq=w_cq_hbm, w_cout=w_cout_hbm,
        w_up=w_up_hbm, w_down=w_down_hbm,
    )
    loads = Bag(
        {
            name: pltpu.make_async_copy(source, getattr(refs, name), refs.load_sem.at[index])
            for index, (name, source) in enumerate(sources.items())
        }
    )
    for name in sources:
        getattr(loads, name).start()

    outs = dict(
        up0=[(o_up_ref, 0, 0, 1024)],
        up1=[(o_up_ref, 0, 1024, 1024)],
        down0=[(o_down_ref, 0, 0, 512), (o_down_ref, 32, 0, 512)],
        down1=[(o_down_ref, 64, 0, 512), (o_down_ref, 96, 0, 512)],
        cross=[(o_cout_ref, 0, 0, 512), (o_cq_ref, 0, 0, 512)],
        out=[(o_out_ref, 0, 0, 512)],
        ckv=[(o_ckv_ref, 0, 0, 1024)],
        wq=[(o_qkv_ref, 0, 0, 512)],
        wk=[(o_qkv_ref, 0, 512, 512)],
        wv=[(o_qkv_ref, 0, 1024, 512)],
    )
    piece = Bag(
        {
            name: Piece(spot, TURNS[name], Bag(refs.pieces[name]), outs[name])
            for name in PIECES
        }
    )
    ups, downs = (piece.up0, piece.up1), (piece.down0, piece.down1)

    def put_rows(to, values, column):
        span = values.shape[1]
        split = values.astype(LOW).reshape(ROWS, 2, 2, 2, HALF, span)
        for half in range(2):
            to.part[half, :, :, :, :, column : column + span] = split[:, :, :, half]

    few_ref = refs.few_sum
    few_ref[...] = jnp.zeros_like(few_ref)

    def few(row, values):
        few_ref[row : row + 1, :] = values

    def gain(row):
        return gains_ref[row : row + 1, :]

    def bias(row):
        return biases_ref[row : row + 1, :]

    send_ref = refs.head_send
    loads.w_qkv.wait()
    zeros_row = jnp.zeros((1, width), WIDE)
    pair_rows, last_rows = slice(0, 2 * head), slice(2 * head, 3 * head)
    pair_land, last_land = refs.pair_land, refs.last_land
    to_heads_copy = Exchange(
        spot, send_ref, refs.to_heads_sem,
        [(block, 1, pair_rows, pair_land, pair_rows) for block in range(own_blocks)]
        + [(0, own_blocks, last_rows, last_land, slice(0, head))],
    )
    pair_bias = jnp.concatenate([bias(0), zeros_row], axis=1)
    for block in range(own_blocks):
        rows = slice(block * BLK, (block + 1) * BLK)
        projected = (nn(tokens_ref[rows, :], refs.w_qkv[:, : 2 * width]) + pair_bias).astype(LOW)
        turned = projected.astype(WIDE).T
        turned = jnp.concatenate([turned[:width] * score_scale, turned[width:]], axis=0).astype(LOW)
        for h in range(HEADS):
            for kind in range(2):
                at = kind * width + h * head
                send_ref[h, block, kind * head : (kind + 1) * head, :] = turned[at : at + head]
        if block == 0:
            pl.semaphore_wait(pltpu.get_barrier_semaphore(), greeted)
        to_heads_copy.start(block)
    for block in range(own_blocks):
        rows = slice(block * BLK, (block + 1) * BLK)
        turned = swap((nn(tokens_ref[rows, :], refs.w_qkv[:, 2 * width :]) + bias(1)).astype(LOW))
        for h in range(HEADS):
            send_ref[h, block, last_rows, :] = turned[h * head : (h + 1) * head]
    to_heads_copy.start(own_blocks)
    all_ref = refs.memory_all
    all_ref[spot.col, spot.row] = memory_ref[...]

    def pass_on(step):
        row = lax.rem(spot.row + ROWS - step, ROWS)
        copy = remote(
            all_ref.at[spot.col, row], all_ref.at[spot.col, row],
            refs.spread_sem.at[0, ROWS + step], refs.spread_sem.at[1, ROWS + step], spot.col_peer,
        )
        copy.start()
        return copy

    passed = [pass_on(0)]
    inv_ref = refs.inverse
    for pos in range(blocks):
        row = jnp.int32(0)
        for other in range(1, blocks):
            row = jnp.where(deal_ref[other] == pos, other, row)
        inv_ref[pos] = row
    for block in range(own_blocks):
        to_heads_copy.wait(block)

    q_ref, kv_ref = refs.q, refs.kv
    no_head = jnp.zeros((head, BLK), LOW)
    no_tile = jnp.zeros((head, TILE), LOW)
    qt_ref, kt_ref, vt_ref = refs.qt, refs.kt, refs.vt
    exact_ref, lse_ref = refs.exact, refs.lse
    for pos in range(blocks):
        block = pair_land[inv_ref[pos]]
        at = slice(pos * BLK, (pos + 1) * BLK)
        qt_ref[:, at] = block[:head]
        kt_ref[:, at] = block[head:]
        kv_ref[at, :] = swap(jnp.concatenate([block[head:], no_head], axis=0))

    prompt_chunks = prompt_blocks * BLK // KEYS
    group = KEYS // TILE

    def key_spans(chunk, tile, step, state):
        base = 0 if chunk < prompt_chunks else prompt_chunks
        lead = tile * TILE - chunk * KEYS
        state = step(chunk, state, lambda s, c: hide_later(s, lead))
        for other in range(base, chunk):
            state = step(other, state, lambda s, c: s)
        for other in range(base):
            state = step(
                other,
                state,
                lambda s, c: hide_prompt(s, offset_ref, open_ref, tile, c, prompt_blocks),
            )
        return state

    def top_tile(chunk, tile):
        here = pl.ds(pl.multiple_of(tile * TILE, TILE), TILE)
        queries = jnp.concatenate([qt_ref[:, here], no_tile], axis=0)

        def top_step(other, top, hide):
            scores = nn(kv_ref[other * KEYS : (other + 1) * KEYS, :], queries)
            scores = hide(scores, other).reshape(KEYS // 8, 8, TILE)
            return jnp.maximum(top, jnp.max(scores, axis=0))

        top = key_spans(chunk, tile, top_step, jnp.full((8, TILE), NEG_FILL, WIDE))
        lse_ref[:, here] = jnp.max(top, axis=0, keepdims=True)

    def each_tile(chunk, step):
        def body(tile, carry):
            step(chunk, tile)
            return carry

        lax.fori_loop(chunk * group, (chunk + 1) * group, body, 0)

    for chunk in range(tiles // group):
        each_tile(chunk, top_tile)
    to_heads_copy.wait(own_blocks)
    spread = []
    for step in range(1, ROWS):
        copy = remote(
            memory_ref, all_ref.at[spot.col, spot.row],
            refs.spread_sem.at[0, step], refs.spread_sem.at[1, step], spot.row_peers[step],
        )
        copy.start()
        spread.append(copy)
    for pos in range(blocks):
        vt_ref[:, pos * BLK : (pos + 1) * BLK] = last_land[inv_ref[pos]]

    def tile_spans(tile, chunk_step, state):
        state = chunk_step(tile, state, lambda s, c: hide_later(s, 0))
        first = jnp.where(tile >= prompt_tiles, prompt_tiles, 0)
        state = lax.fori_loop(first, tile, lambda c, s: chunk_step(c, s, lambda x, _: x), state)
        return lax.fori_loop(
            0,
            first,
            lambda c, s: chunk_step(
                c, s, lambda x, cc: hide_prompt(x, offset_ref, open_ref, tile, cc, prompt_blocks)
            ),
            state,
        )

    def mix_tile(chunk, tile):
        here = pl.ds(pl.multiple_of(tile * TILE, TILE), TILE)
        queries = jnp.concatenate([qt_ref[:, here], no_tile], axis=0)
        top = lse_ref[:, here]

        def mix_step(other, state, hide):
            total, mixed = state
            there = slice(other * KEYS, (other + 1) * KEYS)
            weights = jnp.exp(hide(nn(kv_ref[there, :], queries), other) - top)
            total = total + jnp.sum(weights.reshape(KEYS // 8, 8, TILE), axis=0)
            return total, mixed + nn(vt_ref[:, there], weights.astype(LOW))

        total, mixed = key_spans(
            chunk, tile, mix_step, (jnp.zeros((8, TILE), WIDE), jnp.zeros((head, TILE), WIDE))
        )
        total = jnp.sum(total, axis=0, keepdims=True)
        exact = mixed / total
        for sub in range(TILE // BLK):
            exact_ref[tile * (TILE // BLK) + sub] = exact[:, sub * BLK : (sub + 1) * BLK]
        lse_ref[:, here] = top + jnp.log(total)

    for chunk in range(tiles // group):
        if chunk == tiles // group - 1:
            spread[0].wait()
            passed.append(pass_on(1))
        each_tile(chunk, mix_tile)
    for step in range(2, ROWS):
        spread[step - 1].wait()
        passed.append(pass_on(step))
    mixed_ref = refs.mixed_send
    for row in range(blocks):
        mixed_ref[row // own_blocks, row % own_blocks] = exact_ref[deal_ref[row]].astype(LOW)
    all_rows = slice(0, head)
    from_heads_copy = Exchange(
        spot, mixed_ref, refs.from_heads_sem,
        [(0, own_blocks, all_rows, refs.mixed_land, all_rows)],
    )
    from_heads_copy.start()

    for pos in range(blocks):
        at = slice(pos * BLK, (pos + 1) * BLK)
        kv_ref[at, :] = swap(jnp.concatenate([kt_ref[:, at], vt_ref[:, at]], axis=0))

    ck_ref, cv_ref, ckt_ref, cvt_ref = refs.ck, refs.cv, refs.ckt, refs.cvt
    loads.w_ckv.wait()

    def encode(col, row):
        rows = pl.ds(pl.multiple_of((row * 2 + col) * mem_rows, mem_rows), mem_rows)
        both = nn(all_ref[col, row], refs.w_ckv[...])
        keys = both[:, :width].astype(LOW)
        values = (both[:, width:] + bias(5)).astype(LOW)
        ck_ref[rows, :] = keys
        cv_ref[rows, :] = values
        ckt_ref[:, rows] = swap(keys)
        cvt_ref[:, rows] = swap(values)

    for row in range(ROWS):
        encode(spot.col, row)
    for copy in passed:
        copy.wait()
    for row in range(ROWS):
        encode(1 - spot.col, row)

    loads.w_out.wait()
    from_heads_copy.wait()
    attended_t_ref = refs.attended_t
    unit_one_ref, unit_two_ref = refs.unit_one, refs.unit_two
    low_one_ref, low_two_ref = refs.low_one, refs.low_two
    for block in range(own_blocks):
        at = slice(block * BLK, (block + 1) * BLK)
        for h in range(HEADS):
            attended_t_ref[h * head : (h + 1) * head, at] = refs.mixed_land[h * own_blocks + block]
    cq_ref, cqt_ref = refs.cq, refs.cqt
    loads.w_cq.wait()

    def rows_at(block):
        return pl.ds(pl.multiple_of(block * BLK, BLK), BLK)

    def first_norm(block, carry):
        rows = rows_at(block)
        attended = swap(attended_t_ref[:, rows])
        first_sum = tokens_ref[rows, :].astype(WIDE) + nn(attended, refs.w_out[...]) + bias(2)
        unit, scale = norm_parts(first_sum)
        unit_one_ref[rows, :] = unit
        refs.scale_one[rows, :] = scale
        low_one = (unit * gain(0) + bias(3)).astype(LOW)
        low_one_ref[rows, :] = low_one
        cross_query = (nn(low_one, refs.w_cq[...]) + bias(4)).astype(LOW).astype(WIDE)
        cross_query = cross_query * score_scale
        cq_ref[rows, :] = cross_query.astype(LOW)
        cqt_ref[:, rows] = cross_query.T.astype(LOW)
        return carry

    lax.fori_loop(0, own_blocks, first_norm, 0)

    pair_width = 2 * head
    cross_exact_ref, cross_lse_ref = refs.cross_exact, refs.cross_lse
    steps = mem_total // STEP

    def pair_at(pair):
        return pl.ds(pl.multiple_of(pair * pair_width, pair_width), pair_width)

    def step_at(step):
        return pl.ds(pl.multiple_of(step * STEP, STEP), STEP)

    def cross_forward(h, carry):
        lanes = pair_at(h // 2)
        at = pl.ds(pl.multiple_of(h * head, head), head)
        own_rows = lax.broadcasted_iota(jnp.int32, (pair_width, row_count), 0) // head
        queries = jnp.where(own_rows == lax.rem(h, 2), cqt_ref[lanes, :].astype(WIDE), 0.0)
        queries = queries.astype(LOW)

        def first_pass(step, top):
            scores = nn(ck_ref[step_at(step), lanes], queries)
            return jnp.maximum(top, jnp.max(scores.reshape(STEP // 8, 8, row_count), axis=0))

        top = lax.fori_loop(
            0, steps, first_pass, jnp.full((8, row_count), NEG_FILL, WIDE), unroll=True
        )
        top = jnp.max(top, axis=0, keepdims=True)

        def second_pass(step, state):
            total, mixed = state
            weights = jnp.exp(nn(ck_ref[step_at(step), lanes], queries) - top)
            total = total + jnp.sum(weights.reshape(STEP // 8, 8, row_count), axis=0)
            return total, mixed + nn(cvt_ref[at, step_at(step)], weights.astype(LOW))

        total, mixed = lax.fori_loop(
            0, steps, second_pass,
            (jnp.zeros((8, row_count), WIDE), jnp.zeros((head, row_count), WIDE)), unroll=True,
        )
        total = jnp.sum(total, axis=0, keepdims=True)
        cross_lse_ref[h] = top + jnp.log(total)
        cross_exact_ref[at, :] = mixed / total
        return carry

    lax.fori_loop(0, HEADS, cross_forward, 0)
    cross_low_ref = refs.cross_low
    total_ref, hidden_ref, slope_ref = g_stream_ref, refs.hidden, refs.slope
    loads.w_cout.wait()

    def second_norm(block, carry):
        rows = rows_at(block)
        cross_low = cross_exact_ref[:, rows].T.astype(LOW)
        cross_low_ref[rows, :] = cross_low
        normed_one = unit_one_ref[rows, :] * gain(0) + bias(3)
        unit, scale = norm_parts(normed_one + nn(cross_low, refs.w_cout[...]) + bias(6))
        unit_two_ref[rows, :] = unit
        refs.scale_two[rows, :] = scale
        normed_two = unit * gain(1) + bias(7)
        low_two_ref[rows, :] = normed_two.astype(LOW)
        total_ref[rows, :] = normed_two + bias(8)
        return carry

    lax.fori_loop(0, own_blocks, second_norm, 0)

    loads.w_up.wait()
    loads.w_down.wait()
    w_up_ref, w_down_ref = refs.w_up, refs.w_down

    def chunk_at(chunk):
        return pl.ds(pl.multiple_of(chunk * width, width), width)

    def up_step(chunk, carry):
        pre = nn(low_two_ref[...], w_up_ref[:, chunk_at(chunk)]) + b_up_ref[:, chunk_at(chunk)]
        normal = 0.5 + 0.5 * lax.erf(pre * (2.0**-0.5))
        hidden = (pre * normal).astype(LOW)
        hidden_ref[chunk] = hidden
        slope = normal + pre * jnp.exp(-0.5 * pre * pre) * ((2.0 * jnp.pi) ** -0.5)
        slope_ref[chunk] = slope.astype(LOW)
        total_ref[...] += nn(hidden, w_down_ref[chunk_at(chunk), :])
        return carry

    lax.fori_loop(0, chunks, up_step, 0)

    low_third_ref = refs.low_third
    no_sums = (zeros_row, zeros_row, zeros_row)

    def third_norm(block, sums):
        rows = rows_at(block)
        unit, scale = norm_parts(total_ref[rows, :])
        output_ref[rows, :] = unit * gain(2) + bias(9)
        upstream = cot_ref[rows, :].astype(WIDE)
        grad = norm_pull(unit, scale, gain(2), upstream)
        low = grad.astype(LOW)
        low_third_ref[rows, :] = low
        total_ref[rows, :] = grad
        return (
            sums[0] + column_sums(upstream * unit),
            sums[1] + column_sums(upstream),
            sums[2] + column_sums(low),
        )

    sums = lax.fori_loop(0, own_blocks, third_norm, no_sums)
    few(6, sums[0])
    few(16, sums[1])
    few(15, sums[2])

    turned_ref = refs.turned
    turned_ref[...] = swap(low_two_ref[...])
    for chunk in range(chunks):
        rows = slice(chunk * width, (chunk + 1) * width)
        grad_hidden = nt(low_third_ref[...], w_down_ref[rows, :])
        grad_pre = (grad_hidden * slope_ref[chunk].astype(WIDE)).astype(LOW)
        few(chunk, column_sums(grad_pre))
        total_ref[...] += nt(grad_pre, w_up_ref[:, rows])
        grad_up = nn(turned_ref[...], grad_pre)
        put_rows(ups[chunk // 2], grad_up, (chunk % 2) * width)
        if chunk % 2 == 1:
            ups[chunk // 2].step()
        if chunk == 2:
            piece.up0.step()
        grad_down = nn(swap(hidden_ref[chunk]), low_third_ref[...])
        split = grad_down.astype(LOW).reshape(2, 2, 4, 2, HALF, width)
        for part in range(4):
            to = downs[part // 2].part
            column = (part % 2) * width
            for half in range(2):
                to[half, chunk, :, :, :, column : column + width] = split[:, :, part, half]
    piece.down0.step()
    piece.down1.step()

    dco_ref, dcot_ref = refs.dco, refs.dcot

    def second_back(block, sums):
        rows = rows_at(block)
        upstream = total_ref[rows, :]
        unit = unit_two_ref[rows, :]
        grad = norm_pull(unit, refs.scale_two[rows, :], gain(1), upstream)
        low = grad.astype(LOW)
        total_ref[rows, :] = grad
        low_third_ref[rows, :] = low
        dco_ref[rows, :] = nt(low, refs.w_cout[...]).astype(LOW)
        dcot_ref[:, rows] = nt(refs.w_cout[...], low).astype(LOW)
        return (
            sums[0] + column_sums(upstream * unit),
            sums[1] + column_sums(upstream),
            sums[2] + column_sums(low),
        )

    sums = lax.fori_loop(0, own_blocks, second_back, no_sums)
    few(5, sums[0])
    few(14, sums[1])
    few(13, sums[2])
    put_rows(piece.cross, nn(swap(cross_low_ref[...]), low_third_ref[...]), 0)
    piece.up1.step()
    piece.down0.step()
    piece.down1.step()

    dcqt_ref = refs.dcqt
    def cross_backward(pair, carry):
        lanes = pair_at(pair)
        low_half = pl.ds(pl.multiple_of(pair * pair_width, head), head)
        high_half = pl.ds(pl.multiple_of(pair * pair_width + head, head), head)
        queries_t = apart(cqt_ref[low_half, :], cqt_ref[high_half, :])
        upstream_t = apart(dcot_ref[low_half, :], dcot_ref[high_half, :])
        queries = apart_columns(cq_ref[:, lanes])
        upstream = apart_columns(dco_ref[:, lanes])
        dots = cross_exact_ref[lanes, :] * dcot_ref[lanes, :].astype(WIDE)
        delta = jnp.concatenate(
            [column_sums(dots[:head]), column_sums(dots[head:])], axis=1
        )
        lse = jnp.concatenate([cross_lse_ref[2 * pair], cross_lse_ref[2 * pair + 1]], axis=1)
        dcqt_ref[lanes, :] = jnp.zeros((pair_width, row_count), WIDE)

        def backward_step(step, carry):
            there = step_at(step)
            weights = jnp.exp(nn(ck_ref[there, lanes], queries_t) - lse)
            grad_weights = nn(cv_ref[there, lanes], upstream_t)
            grad_scores = (weights * (grad_weights - delta)).astype(LOW)
            ck_ref[there, lanes] = nn(grad_scores, queries).astype(LOW)
            cv_ref[there, lanes] = nn(weights.astype(LOW), upstream).astype(LOW)
            dcqt_ref[low_half, :] += nn(ckt_ref[low_half, there], grad_scores[:, :row_count])
            dcqt_ref[high_half, :] += nn(ckt_ref[high_half, there], grad_scores[:, row_count:])
            return carry

        lax.fori_loop(0, steps, backward_step, 0)
        return carry

    lax.fori_loop(0, pairs, cross_backward, 0)
    upstream_send = refs.mixed_send

    def first_back(block, sums):
        rows = rows_at(block)
        grad_cq = (dcqt_ref[:, rows].T * score_scale).astype(LOW)
        dco_ref[rows, :] = grad_cq
        upstream = total_ref[rows, :] + nt(grad_cq, refs.w_cq[...])
        unit = unit_one_ref[rows, :]
        grad = norm_pull(unit, refs.scale_one[rows, :], gain(0), upstream)
        low = grad.astype(LOW)
        total_ref[rows, :] = grad
        low_third_ref[rows, :] = low
        grad_attended_t = nt(refs.w_out[...], low).astype(LOW)
        for h in range(HEADS):
            upstream_send[h, block] = grad_attended_t[h * head : (h + 1) * head, :]
        return (
            sums[0] + column_sums(upstream * unit),
            sums[1] + column_sums(upstream),
            sums[2] + column_sums(low),
            sums[3] + column_sums(grad_cq),
        )

    sums = lax.fori_loop(0, own_blocks, first_back, no_sums + (zeros_row,))
    few(4, sums[0])
    few(10, sums[1])
    few(9, sums[2])
    few(11, sums[3])
    up_heads_copy = Exchange(
        spot, upstream_send, refs.up_heads_sem,
        [(0, own_blocks, all_rows, refs.up_land, all_rows)],
    )
    up_heads_copy.start()
    turned_ref[...] = swap(low_one_ref[...])
    put_rows(piece.cross, nn(turned_ref[...], dco_ref[...]), width)
    piece.cross.steps(1)
    put_rows(piece.out, nn(attended_t_ref[...], low_third_ref[...]), 0)
    piece.out.steps(1)
    for part in range(HEADS):
        rows = slice(part * mem_rows, (part + 1) * mem_rows)
        ckt_ref[:, rows] = swap(all_ref[part % 2, part // 2])
        grad = nt(ck_ref[rows, :], refs.w_ckv[:, :width]) + nt(cv_ref[rows, :], refs.w_ckv[:, width:])
        w_up_ref[
            (part // 2) * mem_rows : (part // 2 + 1) * mem_rows,
            (part % 2) * width : (part % 2 + 1) * width,
        ] = grad.astype(LOW)
    g_land = refs.memory_land
    other_side = pl.ds(pl.multiple_of((1 - spot.col) * width, width), width)
    own_side = pl.ds(pl.multiple_of(spot.col * width, width), width)
    memory_copy = remote(
        w_up_ref.at[:, other_side], g_land, refs.memory_sem.at[0, 0], refs.memory_sem.at[1, 0],
        spot.col_peer,
    )
    put_rows(piece.ckv, nn(ckt_ref[...], ck_ref[...]), 0)
    put_rows(piece.ckv, nn(ckt_ref[...], cv_ref[...]), width)
    few(12, column_sums(cv_ref[...]))
    piece.ckv.steps(1)
    for pos in range(blocks):
        at = slice(pos * BLK, (pos + 1) * BLK)
        q_ref[at, :] = swap(jnp.concatenate([qt_ref[:, at], no_head], axis=0))
    up_heads_copy.wait()
    for item in ups + downs:
        item.steps(3)
    memory_copy.start()
    for item in (piece.cross, piece.out, piece.ckv):
        item.steps(2)

    upq_ref, upt_ref = refs.up, refs.upt
    dkv_ref, dqt_ref = refs.dkv, refs.dqt
    for pos in range(blocks):
        block = refs.up_land[inv_ref[pos]]
        at = slice(pos * BLK, (pos + 1) * BLK)
        upt_ref[:, at] = block
        upq_ref[at, :] = swap(jnp.concatenate([no_head, block], axis=0))
    dkv_ref[...] = jnp.zeros_like(dkv_ref)

    def backward_tile(tile, carry):
        here = pl.ds(pl.multiple_of(tile * TILE, TILE), TILE)
        queries_t = jnp.concatenate([qt_ref[:, here], no_tile], axis=0)
        upstream_t = jnp.concatenate([no_tile, upt_ref[:, here]], axis=0)
        both = jnp.concatenate([q_ref[here, :], upq_ref[here, :]], axis=0)
        lse = lse_ref[:, here]
        exact = jnp.concatenate(
            [exact_ref[tile * (TILE // BLK) + sub] for sub in range(TILE // BLK)], axis=1
        )
        delta = column_sums(exact * upt_ref[:, here].astype(WIDE))

        def chunk_step(chunk, grad_q, hide):
            there = pl.ds(pl.multiple_of(chunk * TILE, TILE), TILE)
            scores = hide(nn(kv_ref[there, :], queries_t), chunk)
            weights = jnp.exp(scores - lse)
            grad_weights = nn(kv_ref[there, :], upstream_t)
            grad_scores = (weights * (grad_weights - delta)).astype(LOW)
            sides = jnp.concatenate([grad_scores, weights.astype(LOW)], axis=1)
            spread_at = pl.ds(chunk * (TILE // BLK), TILE // BLK)
            dkv_ref[spread_at] += nn(sides, both).reshape(TILE // BLK, BLK, 2 * head)
            return grad_q + nn(kt_ref[:, there], grad_scores)

        grad_q = tile_spans(tile, chunk_step, jnp.zeros((head, TILE), WIDE))
        grad_q = (grad_q * score_scale).astype(LOW)
        for sub in range(TILE // BLK):
            dqt_ref[tile * (TILE // BLK) + sub] = grad_q[:, sub * BLK : (sub + 1) * BLK]
        return carry

    lax.fori_loop(0, tiles // 2, backward_tile, 0)
    for item in ups + downs:
        item.steps(4)
    lax.fori_loop(tiles // 2, tiles, backward_tile, 0)

    back_send = refs.head_send
    back_copy = Exchange(
        spot, back_send, refs.back_sem,
        [
            (0, own_blocks, slice(0, head), pair_land, slice(0, head)),
            (0, own_blocks, slice(head, 2 * head), pair_land, slice(head, 2 * head)),
            (0, own_blocks, last_rows, last_land, slice(0, head)),
        ],
    )
    for row in range(blocks):
        back_send[row // own_blocks, row % own_blocks, :head] = dqt_ref[deal_ref[row]]
    back_copy.start(0)
    for row in range(blocks):
        back_send[row // own_blocks, row % own_blocks, head:] = dkv_ref[deal_ref[row]].T.astype(LOW)
    back_copy.start(1)
    back_copy.start(2)

    ones = jnp.ones((8, BLK), LOW)
    query_sums = jnp.zeros((8, head), WIDE)
    both_sums = jnp.zeros((1, 2 * head), WIDE)
    for pos in range(blocks):
        query_sums = query_sums + nt(ones, dqt_ref[pos])
        both_sums = both_sums + column_sums(dkv_ref[pos])
    own_lanes = lax.broadcasted_iota(jnp.int32, (1, width), 1) // head == spot.ctx
    few(7, jnp.where(own_lanes, jnp.concatenate([query_sums[:1]] * HEADS, axis=1), 0.0))
    few(8, jnp.where(own_lanes, jnp.concatenate([both_sums[:, head:]] * HEADS, axis=1), 0.0))

    few_core, few_plane, few_rows = refs.few_core, refs.few_plane, refs.few_rows
    few_sem = refs.few_sem
    core_copy = remote(few_ref, few_core, few_sem.at[0, 0], few_sem.at[1, 0], spot.core_peer)
    core_copy.start()
    for item in ups + downs:
        item.steps(5)
    core_copy.wait()
    own_place = spot.col * 2 + spot.wsh
    few_plane[own_place] = few_ref[...] + few_core[...]
    plane_copies = []
    for way, (target, _, _) in enumerate(spot.ways):
        copy = remote(
            few_plane.at[own_place], few_plane.at[own_place],
            few_sem.at[0, 1 + way], few_sem.at[1, 1 + way], target,
        )
        copy.start()
        plane_copies.append(copy)
    piece.cross.steps(3)
    piece.out.steps(3)
    for copy in plane_copies:
        copy.wait()
    few_rows[spot.row] = few_plane[0] + few_plane[1] + few_plane[2] + few_plane[3]
    row_copies = []
    for step in range(1, ROWS):
        copy = remote(
            few_rows.at[spot.row], few_rows.at[spot.row],
            few_sem.at[0, 3 + step], few_sem.at[1, 3 + step], spot.row_peers[step],
        )
        copy.start()
        row_copies.append(copy)
    piece.ckv.steps(3)
    memory_copy.wait()
    g_land[...] = plus(w_up_ref[:, own_side], g_land[...]).astype(LOW)
    for item in ups + downs:
        item.steps(6)

    turned_ref[...] = swap(tokens_ref[...])
    kinds = (piece.wq, piece.wk, piece.wv)
    for kind in range(3):
        back_copy.wait(kind)
        for block in range(own_blocks):
            turned = jnp.concatenate(
                [
                    (pair_land, pair_land, last_land)[kind][
                        h * own_blocks + block, kind % 2 * head : (kind % 2 + 1) * head, :
                    ]
                    for h in range(HEADS)
                ],
                axis=0,
            )
            hidden_ref[kind, block * BLK : (block + 1) * BLK, :] = swap(turned)
        put_rows(kinds[kind], nn(turned_ref[...], hidden_ref[kind]), 0)
        kinds[kind].steps(1)
        if kind > 0:
            kinds[kind - 1].steps(2)
    for item in (piece.cross, piece.out, piece.ckv):
        item.steps(4)
    memory_copies = []
    for step in range(1, ROWS):
        copy = remote(
            g_land.at[pl.ds(spot.rows_by_step[step] * mem_rows, mem_rows)], refs.memory_row.at[step - 1],
            refs.memory_sem.at[0, step], refs.memory_sem.at[1, step], spot.row_peers[step],
        )
        copy.start()
        memory_copies.append(copy)
    grad_stream = total_ref[...]
    for kind in range(3):
        if kind == 1:
            kinds[2].steps(2)
        lanes = slice(kind * width, (kind + 1) * width)
        grad_stream = grad_stream + nt(hidden_ref[kind], refs.w_qkv[:, lanes])
    g_stream_ref[...] = grad_stream
    for item in kinds:
        item.steps(3)
    for copy in row_copies:
        copy.wait()
    total = few_rows[0] + few_rows[1] + few_rows[2] + few_rows[3]
    own_shard = spot.ctx * 2 + spot.wsh
    part, long_part = width // SHARDS, hidden_width // SHARDS
    picked, long_picked = total[:, :part], total[:1, :long_part]
    for shard in range(1, SHARDS):
        picked = jnp.where(own_shard == shard, total[:, shard * part : (shard + 1) * part], picked)
        row, at = divmod(shard * long_part, width)
        long_picked = jnp.where(
            own_shard == shard, total[row : row + 1, at : at + long_part], long_picked
        )
    o_b_up_ref[...] = long_picked
    o_gains_ref[...] = picked[4:7]
    o_biases_ref[...] = picked[7:17]
    for item in (piece.cross, piece.out, piece.ckv):
        item.steps(5)
    for copy in memory_copies:
        copy.wait()
    total = g_land[pl.ds(spot.row * mem_rows, mem_rows), :].astype(WIDE)
    for step in range(ROWS - 1):
        total = total + refs.memory_row[step].astype(WIDE)
    g_memory_ref[...] = total
    for item in kinds + (piece.cross, piece.out, piece.ckv):
        item.steps(6)


def layer_scratch(row_count, width, hidden_width, mem_rows):
    own_blocks = row_count // BLK
    blocks = own_blocks * HEADS
    head = width // HEADS
    tokens = blocks * BLK
    mem_total = mem_rows * HEADS
    dma = pltpu.SemaphoreType.DMA
    scratch = dict(
        w_qkv=((width, 3 * width), LOW), w_ckv=((width, 2 * width), LOW),
        w_out=((width, width), LOW), w_cq=((width, width), LOW),
        w_cout=((width, width), LOW), w_up=((width, hidden_width), LOW),
        w_down=((hidden_width, width), LOW),
        head_send=((HEADS, own_blocks, 3 * head, BLK), LOW),
        pair_land=((blocks, 2 * head, BLK), LOW), last_land=((blocks, head, BLK), LOW),
        memory_all=((2, ROWS, mem_rows, width), LOW),
        q=((tokens, 2 * head), LOW), kv=((tokens, 2 * head), LOW),
        qt=((head, tokens), LOW), kt=((head, tokens), LOW), vt=((head, tokens), LOW),
        exact=((blocks, head, BLK), WIDE), lse=((1, tokens), WIDE),
        mixed_send=((HEADS, own_blocks, head, BLK), LOW),
        mixed_land=((blocks, head, BLK), LOW),
        ck=((mem_total, width), LOW), cv=((mem_total, width), LOW),
        ckt=((width, mem_total), LOW), cvt=((width, mem_total), LOW),
        attended_t=((width, row_count), LOW),
        unit_one=((row_count, width), WIDE), unit_two=((row_count, width), WIDE),
        scale_one=((row_count, 1), WIDE), scale_two=((row_count, 1), WIDE),
        low_one=((row_count, width), LOW), low_two=((row_count, width), LOW),
        cq=((row_count, width), LOW), cqt=((width, row_count), LOW),
        cross_exact=((width, row_count), WIDE),
        cross_lse=((HEADS, 1, row_count), WIDE),
        cross_low=((row_count, width), LOW),
        hidden=((hidden_width // width, row_count, width), LOW),
        slope=((hidden_width // width, row_count, width), LOW),
        low_third=((row_count, width), LOW),
        turned=((width, row_count), LOW),
        dco=((row_count, width), LOW), dcot=((width, row_count), LOW),
        dcqt=((width, row_count), WIDE),
        memory_land=((ROWS * mem_rows, width), LOW),
        memory_row=((ROWS - 1, mem_rows, width), LOW),
        up_land=((blocks, head, BLK), LOW),
        up=((tokens, 2 * head), LOW), upt=((head, tokens), LOW),
        dkv=((blocks, BLK, 2 * head), WIDE), dqt=((blocks, head, BLK), LOW),
        few_sum=((FEW_ROWS, width), WIDE), few_core=((FEW_ROWS, width), WIDE),
        few_plane=((4, FEW_ROWS, width), WIDE), few_rows=((ROWS, FEW_ROWS, width), WIDE),
    )
    out = {name: pltpu.VMEM(shape, kind) for name, (shape, kind) in scratch.items()}
    out.update(
        load_sem=dma((7,)), to_heads_sem=dma((2, HEADS, 4)), from_heads_sem=dma((2, HEADS, 1)),
        up_heads_sem=dma((2, HEADS, 1)), back_sem=dma((2, HEADS, 3)), spread_sem=dma((2, 2 * ROWS)),
        inverse=pltpu.SMEM((blocks,), jnp.int32),
        memory_sem=dma((2, ROWS)), few_sem=dma((2, 7)),
    )
    out.update(
        pieces={
            name: dict(
                part=pltpu.VMEM((2, ROWS, 2, 2, HALF, span), LOW),
                core_land=pltpu.VMEM((ROWS, 2, 2, HALF, span), LOW),
                hop_land=pltpu.VMEM(
                    (3, ROWS, HALF, span) if TURNS[name] == 2 else (ROWS, 2, HALF, span), LOW
                ),
                turn_land=pltpu.VMEM((ROWS, HALF, span), LOW),
                row_land=pltpu.VMEM(
                    (2, ROWS, HALF, span) if TURNS[name] == 2 else (ROWS - 1, HALF, span), LOW
                ),
                sems=dma((2, 12)),
            )
            for name, span in PIECES.items()
        }
    )
    return out


def layer_call(deal_ids, offsets, opened, tokens, memory, cotangent, weights, b_up, gains, biases, prompt_blocks):
    row_count, width = tokens.shape
    hidden_width = b_up.shape[1]
    mem_rows = memory.shape[0]
    smem = pl.BlockSpec(memory_space=pltpu.SMEM)
    vmem = pl.BlockSpec(memory_space=pltpu.VMEM)
    hbm = pl.BlockSpec(memory_space=pl.ANY)
    scratch = layer_scratch(row_count, width, hidden_width, mem_rows)
    leaves, tree = jax.tree.flatten(scratch, is_leaf=lambda leaf: not isinstance(leaf, dict))
    out_shapes = [
        (row_count, width), (row_count, width), (mem_rows, width),
        (32, 3 * width), (32, width), (32, width), (32, 2 * width), (32, width),
        (32, hidden_width), (hidden_width // SHARDS, width),
        (1, hidden_width // SHARDS), (3, width // SHARDS), (10, width // SHARDS),
    ]

    def body(*args):
        count = len(args) - len(leaves)
        refs = Bag(jax.tree.unflatten(tree, args[count:]))
        layer_kernel(prompt_blocks, *args[:count], refs)

    return pl.pallas_call(
        body,
        out_shape=[jax.ShapeDtypeStruct(shape, WIDE) for shape in out_shapes],
        in_specs=[smem] * 3 + [vmem] * 3 + [hbm] * 7 + [vmem] * 3,
        out_specs=[vmem] * len(out_shapes),
        scratch_shapes=leaves,
        compiler_params=pltpu.CompilerParams(
            collective_id=0, has_side_effects=True, vmem_limit_bytes=BIG_VMEM
        ),
        name="layer",
    )(deal_ids, offsets, opened, tokens, memory, cotangent, *weights, b_up, gains, biases)


def hand_out_kernel(count, *refs):
    for index in range(count):
        refs[count + index][...] = refs[index][...]


def hand_out(arrays):
    count = len(arrays)
    vmem = pl.BlockSpec(memory_space=pltpu.VMEM)
    return pl.pallas_call(
        functools.partial(hand_out_kernel, count),
        out_shape=[jax.ShapeDtypeStruct(a.shape, a.dtype) for a in arrays],
        in_specs=[vmem] * count,
        out_specs=[vmem] * count,
        compiler_params=pltpu.CompilerParams(vmem_limit_bytes=BIG_VMEM),
        name="hand_out",
    )(*arrays)


def layer_shards(
    stream, memory, cotangent, deal_order, offsets, context_mask,
    w_qkv, w_out, w_cq, w_ckv, w_cout, w_up, w_down, b_up, gains, biases,
):
    results = layer_call(
        deal_order[0, 0], offsets[0, 0], context_mask[0, 0],
        stream[0, 0], memory[0, 0], cotangent[0, 0],
        (w_qkv, w_out, w_cq, w_ckv, w_cout, w_up, w_down),
        b_up[None, :], gains, biases, context_mask.shape[3],
    )
    output, grad_stream, grad_memory, *grads = hand_out(results)
    grads[7] = grads[7].reshape(-1)
    return (output[None, None], grad_stream[None, None], grad_memory[None, None], *grads)


def gelu_exact(values):
    return jax.nn.gelu(values, approximate=False)


def norm_rows(values, gain_vec, shift_vec):
    center = values - jnp.mean(values, axis=-1, keepdims=True)
    spread = jnp.mean(center * center, axis=-1, keepdims=True)
    return center * lax.rsqrt(spread + EPS_NORM) * gain_vec + shift_vec


def norm_back(values, gain_vec, shift_vec, upstream):
    _, pullback = jax.vjp(norm_rows, values, gain_vec, shift_vec)
    return pullback(upstream)


def seq_index(positions, prompt_len, cont_len):
    later = jnp.int32(1) + (positions - jnp.int32(prompt_len)) // jnp.int32(cont_len)
    return jnp.where(positions < prompt_len, jnp.zeros_like(later), later)


def visible(query_pos, key_ids, offsets, context_mask, block_len, prompt_blocks, cont_blocks):
    prompt_len = prompt_blocks * block_len
    cont_len = cont_blocks * block_len
    cont_count = offsets.shape[0]
    key_pos = (
        key_ids[:, None] * jnp.int32(block_len) + jnp.arange(block_len, dtype=jnp.int32)[None, :]
    ).reshape(-1)
    query_seq = seq_index(query_pos, prompt_len, cont_len)
    key_seq = seq_index(key_pos, prompt_len, cont_len)
    inside = (query_seq[:, None] == key_seq[None, :]) & (key_pos[None, :] <= query_pos[:, None])
    cont_pick = jnp.clip(query_seq - 1, 0, cont_count - 1)
    prompt_limit = jnp.take(offsets, cont_pick)
    query_block = jnp.clip(
        (query_pos - jnp.int32(prompt_len)) // jnp.int32(block_len), 0, cont_count * cont_blocks - 1
    )
    mask_rows = jnp.take(context_mask, query_block, axis=0)
    key_block = jnp.clip(key_ids, 0, prompt_blocks - 1)
    block_open = jnp.take(mask_rows, key_block, axis=1) > 0
    block_open = jnp.repeat(block_open, block_len, axis=1) | (key_pos[None, :] < block_len)
    from_prompt = (
        (query_seq[:, None] > 0)
        & (key_seq[None, :] == 0)
        & (key_pos[None, :] < prompt_limit[:, None])
        & block_open
    )
    return inside | from_prompt


def dot_first(left, right):
    return lax.dot_general(
        left, right, (((0,), (0,)), ((), ())), preferred_element_type=jnp.float32
    )


def dot_last(left, right):
    return lax.dot_general(
        left, right, (((1,), (1,)), ((), ())), preferred_element_type=jnp.float32
    )


def to_heads(matrix, head_count):
    row_count, model_width = matrix.shape
    return matrix.reshape(row_count, head_count, model_width // head_count).transpose(1, 0, 2)


def from_heads(stacked):
    head_count, row_count, head_width = stacked.shape
    return stacked.transpose(1, 0, 2).reshape(row_count, head_count * head_width)


def pair_heads(key_rows, value_rows, head_count):
    return jnp.concatenate(
        [to_heads(key_rows, head_count), to_heads(value_rows, head_count)], axis=2
    )


def head_scores(queries, key_rows, allowed):
    score_scale = queries.shape[1] ** (-0.5)
    scores = dot_last(queries, key_rows) * score_scale
    if allowed is not None:
        scores = jnp.where(allowed, scores, NEG_FILL)
    return scores


def head_forward(queries, keyval, allowed):
    head_width = queries.shape[1]
    scores = head_scores(queries, keyval[:, :head_width], allowed)
    row_top = jnp.max(scores, axis=1, keepdims=True)
    exp_scores = jnp.exp(scores - row_top)
    row_total = jnp.sum(exp_scores, axis=1, keepdims=True)
    soft_weights = (exp_scores / row_total).astype(jnp.bfloat16)
    mixed_heads = jnp.dot(soft_weights, keyval[:, head_width:], preferred_element_type=jnp.float32)
    return (mixed_heads, row_top + jnp.log(row_total))


def head_backward(queries, keyval, upstream, log_total, allowed):
    head_width = queries.shape[1]
    score_scale = head_width ** (-0.5)
    key_rows = keyval[:, :head_width]
    scores = head_scores(queries, key_rows, allowed)
    soft_weights = jnp.exp(scores - log_total)
    grad_soft = dot_last(upstream, keyval[:, head_width:])
    row_delta = jnp.sum(soft_weights * grad_soft, axis=1, keepdims=True)
    grad_scores = (soft_weights * (grad_soft - row_delta)).astype(jnp.bfloat16)
    grad_query = jnp.dot(grad_scores, key_rows, preferred_element_type=jnp.float32) * score_scale
    grad_keys = dot_first(grad_scores, queries) * score_scale
    grad_values = dot_first(soft_weights.astype(jnp.bfloat16), upstream)
    return (grad_query, jnp.concatenate([grad_keys, grad_values], axis=1))


def shards(
    stream,
    memory,
    cotangent,
    deal_order,
    offsets,
    context_mask,
    w_qkv,
    w_out,
    w_cq,
    w_ckv,
    w_cout,
    w_up,
    w_down,
    b_up,
    gains,
    biases,
):
    tokens = stream[0, 0]
    row_count, model_width = tokens.shape
    head_width = model_width // HEADS
    deal_ids = deal_order[0, 0]
    prompt_blocks = context_mask.shape[3]
    own_blocks = row_count // BLK
    own_ids = lax.dynamic_slice_in_dim(deal_ids, lax.axis_index("ctx") * own_blocks, own_blocks)
    query_pos = (
        own_ids[:, None] * jnp.int32(BLK) + jnp.arange(BLK, dtype=jnp.int32)[None, :]
    ).reshape(-1)
    allowed = visible(
        query_pos, deal_ids, offsets[0, 0], context_mask[0, 0], BLK, prompt_blocks, CBLK
    )
    zeros_row = jnp.zeros((model_width,), jnp.float32)
    projected = (
        jnp.dot(tokens, w_qkv, preferred_element_type=jnp.float32)
        + jnp.concatenate([biases[0], zeros_row, biases[1]])
    ).astype(jnp.bfloat16)
    query_heads = to_heads(projected[:, :model_width], HEADS)
    keyval_own = pair_heads(
        projected[:, model_width : 2 * model_width], projected[:, 2 * model_width :], HEADS
    )
    keyval_all = lax.all_gather(keyval_own, "ctx", axis=1, tiled=True)

    def self_forward(pieces):
        return head_forward(pieces[0], pieces[1], allowed)

    self_out, self_lse = lax.map(self_forward, (query_heads, keyval_all))
    attended = from_heads(self_out).astype(jnp.bfloat16)
    first_sum = (
        tokens.astype(jnp.float32)
        + jnp.dot(attended, w_out, preferred_element_type=jnp.float32)
        + biases[2]
    )
    normed_one = norm_rows(first_sum, gains[0], biases[3])
    normed_low = normed_one.astype(jnp.bfloat16)
    cross_query = (
        jnp.dot(normed_low, w_cq, preferred_element_type=jnp.float32) + biases[4]
    ).astype(jnp.bfloat16)
    cross_bias = jnp.concatenate([zeros_row, biases[5]])
    memory_own = memory[0, 0]
    memory_all = lax.all_gather(memory_own, "ctx", axis=0, tiled=True)
    cross_kv = (jnp.dot(memory_all, w_ckv, preferred_element_type=jnp.float32) + cross_bias).astype(
        jnp.bfloat16
    )
    cross_heads = pair_heads(cross_kv[:, :model_width], cross_kv[:, model_width:], HEADS)
    cross_query_heads = to_heads(cross_query, HEADS)

    def cross_forward(pieces):
        return head_forward(pieces[0], pieces[1], None)

    cross_out, cross_lse = lax.map(cross_forward, (cross_query_heads, cross_heads))
    cross_attended = from_heads(cross_out).astype(jnp.bfloat16)
    second_sum = (
        normed_one + jnp.dot(cross_attended, w_cout, preferred_element_type=jnp.float32) + biases[6]
    )
    normed_two = norm_rows(second_sum, gains[1], biases[7])
    normed_two_low = normed_two.astype(jnp.bfloat16)
    hidden_pre = jnp.dot(normed_two_low, w_up, preferred_element_type=jnp.float32) + b_up
    hidden = gelu_exact(hidden_pre).astype(jnp.bfloat16)
    third_sum = normed_two + jnp.dot(hidden, w_down, preferred_element_type=jnp.float32) + biases[8]
    output = norm_rows(third_sum, gains[2], biases[9])
    grad_third, grad_gain_three, grad_shift_three = norm_back(
        third_sum, gains[2], biases[9], cotangent[0, 0].astype(jnp.float32)
    )
    grad_down_in = grad_third.astype(jnp.bfloat16)
    grad_w_down = dot_first(hidden, grad_down_in)
    grad_b_down = jnp.sum(grad_down_in.astype(jnp.float32), axis=0)
    grad_hidden = dot_last(grad_down_in, w_down)
    _, gelu_pull = jax.vjp(gelu_exact, hidden_pre)
    grad_pre = gelu_pull(grad_hidden)[0].astype(jnp.bfloat16)
    grad_w_up = dot_first(normed_two_low, grad_pre)
    grad_b_up = jnp.sum(grad_pre.astype(jnp.float32), axis=0)
    grad_normed_two = grad_third + dot_last(grad_pre, w_up)
    grad_second, grad_gain_two, grad_shift_two = norm_back(
        second_sum, gains[1], biases[7], grad_normed_two
    )
    grad_cross_in = grad_second.astype(jnp.bfloat16)
    grad_w_cout = dot_first(cross_attended, grad_cross_in)
    grad_b_co = jnp.sum(grad_cross_in.astype(jnp.float32), axis=0)
    grad_cross_heads = to_heads(dot_last(grad_cross_in, w_cout).astype(jnp.bfloat16), HEADS)

    def cross_backward(pieces):
        return head_backward(pieces[0], pieces[1], pieces[2], pieces[3], None)

    grad_cq_heads, grad_ckv_all = lax.map(
        cross_backward, (cross_query_heads, cross_heads, grad_cross_heads, cross_lse)
    )
    grad_ckv_own = lax.psum_scatter(
        grad_ckv_all.astype(jnp.bfloat16), "ctx", scatter_dimension=1, tiled=True
    )
    grad_cv = from_heads(grad_ckv_own[:, :, head_width:])
    grad_ckv = jnp.concatenate([from_heads(grad_ckv_own[:, :, :head_width]), grad_cv], axis=1)
    grad_w_ckv = dot_first(memory_own, grad_ckv)
    grad_b_cv = jnp.sum(grad_cv.astype(jnp.float32), axis=0)
    grad_memory = dot_last(grad_ckv, w_ckv)
    grad_cq = from_heads(grad_cq_heads).astype(jnp.bfloat16)
    grad_w_cq = dot_first(normed_low, grad_cq)
    grad_b_cq = jnp.sum(grad_cq.astype(jnp.float32), axis=0)
    grad_normed_one = grad_second + dot_last(grad_cq, w_cq)
    grad_first, grad_gain_one, grad_shift_one = norm_back(
        first_sum, gains[0], biases[3], grad_normed_one
    )
    grad_att_in = grad_first.astype(jnp.bfloat16)
    grad_w_out = dot_first(attended, grad_att_in)
    grad_b_o = jnp.sum(grad_att_in.astype(jnp.float32), axis=0)
    grad_self_heads = to_heads(dot_last(grad_att_in, w_out).astype(jnp.bfloat16), HEADS)

    def self_backward(pieces):
        return head_backward(pieces[0], pieces[1], pieces[2], pieces[3], allowed)

    grad_q_heads, grad_kv_all = lax.map(
        self_backward, (query_heads, keyval_all, grad_self_heads, self_lse)
    )
    grad_kv_own = lax.psum_scatter(
        grad_kv_all.astype(jnp.bfloat16), "ctx", scatter_dimension=1, tiled=True
    )
    grad_values = from_heads(grad_kv_own[:, :, head_width:])
    grad_queries = from_heads(grad_q_heads).astype(jnp.bfloat16)
    grad_proj = jnp.concatenate(
        [grad_queries, from_heads(grad_kv_own[:, :, :head_width]), grad_values], axis=1
    )
    grad_w_qkv = dot_first(tokens, grad_proj)
    grad_b_q = jnp.sum(grad_queries.astype(jnp.float32), axis=0)
    grad_b_v = jnp.sum(grad_values.astype(jnp.float32), axis=0)
    grad_tokens = grad_first + dot_last(grad_proj, w_qkv)
    gain_grads = jnp.stack([grad_gain_one, grad_gain_two, grad_gain_three])
    shift_grads = jnp.stack(
        [
            grad_b_q,
            grad_b_v,
            grad_b_o,
            grad_shift_one,
            grad_b_cq,
            grad_b_cv,
            grad_b_co,
            grad_shift_two,
            grad_b_down,
            grad_shift_three,
        ]
    )
    (
        part_qkv,
        part_out,
        part_cq,
        part_ckv,
        part_cout,
        part_up,
        part_down,
        part_b_up,
        part_gains,
        part_biases,
    ) = (
        lax.psum_scatter(grad_w_qkv, ("ctx", "wsh"), scatter_dimension=0, tiled=True),
        lax.psum_scatter(grad_w_out, ("ctx", "wsh"), scatter_dimension=0, tiled=True),
        lax.psum_scatter(grad_w_cq, ("ctx", "wsh"), scatter_dimension=0, tiled=True),
        lax.psum_scatter(grad_w_ckv, ("ctx", "wsh"), scatter_dimension=0, tiled=True),
        lax.psum_scatter(grad_w_cout, ("ctx", "wsh"), scatter_dimension=0, tiled=True),
        lax.psum_scatter(grad_w_up, ("ctx", "wsh"), scatter_dimension=0, tiled=True),
        lax.psum_scatter(grad_w_down, ("ctx", "wsh"), scatter_dimension=0, tiled=True),
        lax.psum_scatter(grad_b_up, ("ctx", "wsh"), scatter_dimension=0, tiled=True),
        lax.psum_scatter(gain_grads, ("ctx", "wsh"), scatter_dimension=1, tiled=True),
        lax.psum_scatter(shift_grads, ("ctx", "wsh"), scatter_dimension=1, tiled=True),
    )
    (
        total_qkv,
        total_out,
        total_cq,
        total_ckv,
        total_cout,
        total_up,
        total_down,
        total_b_up,
        total_gains,
        total_biases,
    ) = (
        lax.psum(part_qkv.astype(jnp.bfloat16), "grp").astype(jnp.float32),
        lax.psum(part_out.astype(jnp.bfloat16), "grp").astype(jnp.float32),
        lax.psum(part_cq.astype(jnp.bfloat16), "grp").astype(jnp.float32),
        lax.psum(part_ckv.astype(jnp.bfloat16), "grp").astype(jnp.float32),
        lax.psum(part_cout.astype(jnp.bfloat16), "grp").astype(jnp.float32),
        lax.psum(part_up.astype(jnp.bfloat16), "grp").astype(jnp.float32),
        lax.psum(part_down.astype(jnp.bfloat16), "grp").astype(jnp.float32),
        lax.psum(part_b_up.astype(jnp.bfloat16), "grp").astype(jnp.float32),
        lax.psum(part_gains.astype(jnp.bfloat16), "grp").astype(jnp.float32),
        lax.psum(part_biases.astype(jnp.bfloat16), "grp").astype(jnp.float32),
    )
    return (
        output[None, None],
        grad_tokens[None, None],
        grad_memory[None, None],
        total_qkv,
        total_out,
        total_cq,
        total_ckv,
        total_cout,
        total_up,
        total_down,
        total_b_up,
        total_gains,
        total_biases,
    )


def solution(mesh):
    in_specs = (
        P("grp", "wsh", "ctx", None),
        P("grp", "wsh", "ctx", None),
        P("grp", "wsh", "ctx", None),
        P("grp", "wsh", None),
        P("grp", "wsh", None),
        P("grp", "wsh", None, None),
        P(),
        P(),
        P(),
        P(),
        P(),
        P(),
        P(),
        P(),
        P(),
        P(),
    )
    out_specs = (
        P("grp", "wsh", "ctx", None),
        P("grp", "wsh", "ctx", None),
        P("grp", "wsh", "ctx", None),
        P(("ctx", "wsh"), None),
        P(("ctx", "wsh"), None),
        P(("ctx", "wsh"), None),
        P(("ctx", "wsh"), None),
        P(("ctx", "wsh"), None),
        P(("ctx", "wsh"), None),
        P(("ctx", "wsh"), None),
        P(("ctx", "wsh")),
        P(None, ("ctx", "wsh")),
        P(None, ("ctx", "wsh")),
    )
    body = layer_shards if mesh.shape["ctx"] == HEADS else shards
    return jax.shard_map(body, mesh=mesh, in_specs=in_specs, out_specs=out_specs, check_vma=False)
```

profile of v0, /device:TPU:0, one launch (start us, length us, event | category | flops | bytes accessed | tf_op | source)
XLA Modules:
  0.0 191.6 jit_solution(7568847336294218313)
XLA Ops:
  1.3 1.4 copy.29.args_2_
  2.6 185.3 %layer.1 = (f32[384,512]{1,0:T(8,128)}, f32[384,512]{1,0:T(8,128)}, f32[128,512]{1,0:T(8,128)}, f32[32,1536]{1,0:T(8,128)}, f32[32,512]{1,0:T(8,128)}, /*index=5...) custom-call(s32[24]{0:T(128)} %bitcast.17, ...), custom_call_target="tpu_custom_call" | custom-call | tf_op jit(solution)/shard_map/layer/pallas_call | solution.py:1100
  188.0 3.4 %hand_out.1 = (f32[384,512]{1,0:T(8,128)}, f32[384,512]{1,0:T(8,128)}, f32[128,512]{1,0:T(8,128)}, f32[32,1536]{1,0:T(8,128)}, f32[32,512]{1,0:T(8,128)}, /*inde...) custom-call(f32[384,512]{1,0:T(8,128)} %get-tuple-element.39.refs_0_, ...), custom_call_target="tpu_custom_call" | custom-call | tf_op jit(solution)/shard_map/hand_out/pallas_call | solution.py:1121
where the time goes:
time: 192 us
  Pallas kernels  189 us (98%)
    pallas_call x1, Pallas kernels, layer_call(): pl.pallas_call(body, out_shape=[jax.ShapeDtypeStruct(shape, WIDE) for sha...  185 us

commit v1 on v0

--- a/solution.py
+++ b/solution.py
@@ -18,7 +18,7 @@
 
 MESH_ID = pl.DeviceIdType.MESH
 TILE = 512
-STEP = 256
+STEP = 512
 KEYS = 1024
 BIG_VMEM = 62 << 20
 LOW = jnp.bfloat16

time: 192 us -> 190 us (0.990)
  Pallas kernels: 189 us -> 187 us
where the time goes in v1:
time: 190 us
  Pallas kernels  187 us (98%)
    pallas_call x1, Pallas kernels, layer_call(): pl.pallas_call(body, out_shape=[jax.ShapeDtypeStruct(shape, WIDE) for sha...  184 us

profile of v1, /device:TPU:0, one launch (start us, length us, event | category | flops | bytes accessed | tf_op | source)
XLA Modules:
  0.0 190.1 jit_solution(8433642179509761445)
XLA Ops:
  1.3 1.4 copy.29.args_2_
  2.6 183.9 %layer.1 = (f32[384,512]{1,0:T(8,128)}, f32[384,512]{1,0:T(8,128)}, f32[128,512]{1,0:T(8,128)}, f32[32,1536]{1,0:T(8,128)}, f32[32,512]{1,0:T(8,128)}, /*index=5...) custom-call(s32[24]{0:T(128)} %bitcast.17, ...), custom_call_target="tpu_custom_call" | custom-call | tf_op jit(solution)/shard_map/layer/pallas_call | solution.py:1100
  186.5 3.4 %hand_out.1 = (f32[384,512]{1,0:T(8,128)}, f32[384,512]{1,0:T(8,128)}, f32[128,512]{1,0:T(8,128)}, f32[32,1536]{1,0:T(8,128)}, f32[32,512]{1,0:T(8,128)}, /*inde...) custom-call(f32[384,512]{1,0:T(8,128)} %get-tuple-element.39.refs_0_, ...), custom_call_target="tpu_custom_call" | custom-call | tf_op jit(solution)/shard_map/hand_out/pallas_call | solution.py:1121
